TPU v7x, 256 devices: a whole 4x4x8 slice. The times are simulated.
256 devices in a mesh: dp: 16 (over x, y), ctx: 16 (over z, core).
Axes of the slice: x: 4, y: 4, z: 8, core: 2. Of those that a mesh axis runs over, the one named last changes fastest.
Arguments:
- queries: bfloat16 [32768, 4096], P(('dp', 'ctx')), parts along dimension 0, may hold values from -180 to 180
- key_states: bfloat16 [32768, 512], P(('dp', 'ctx')), parts along dimension 0, may hold values from -5 to 5
- value_states: bfloat16 [32768, 512], P(('dp', 'ctx')), parts along dimension 0, may hold values from -6 to 6
- grad_output: bfloat16 [32768, 4096], P(('dp', 'ctx')), parts along dimension 0, may hold values from -6 to 6
- doc_ids: int32 [32768], P('dp'), parts along dimension 0, may hold values from 0 to 3, never falling along the last dimension, each value on 1 to 1024 neighbouring positions
Outputs:
- query_grad: bfloat16 [32768, 4096], P(('dp', 'ctx')), parts along dimension 0
- key_grad: bfloat16 [32768, 512], P(('dp', 'ctx')), parts along dimension 0
- value_grad: bfloat16 [32768, 512], P(('dp', 'ctx')), parts along dimension 0
There are 16 independent parts, one for each index of `dp`. A program takes and returns all parts, laid end to end along the dimension named above; each array names one. Nothing has to cross between parts.
Inputs may be any that keep to these rules, and one draw needn't show every extreme that they name: `doc_ids`: never falls along positions; each document holds 1 to 1024 positions and one holds exactly 1024.
All inputs are finite; a program needn't handle non-finite values.
Results may differ from a plain program's by a relative error of at most 0.029.
Values may be sent and summed in bfloat16 or wider, within the bound.
No kernel may reach another device: no remote copies, remote signals or barrier semaphores. Data moves between devices by JAX's collectives and lax.ppermute only.
A program may use at most 128 MiB of HBM per device.

v0:
```python
import jax
import jax.numpy as jnp
from jax import lax
from jax.sharding import PartitionSpec as P

DH = 128
GROUP = 8
KEY_BLOCK = 128


NEG = -1e30


def storage_order(flat, group_size):
    blocks = flat.reshape(2 * group_size, -1)
    return jnp.stack([blocks[:group_size], blocks[group_size:][::-1]], axis=1).reshape(-1)


def visible_of(pos_query, doc_query, pos_key, doc_key):
    return (pos_key[None, :] <= pos_query[:, None]) & (doc_key[None, :] == doc_query[:, None])


def scores_of(query_part, key_block):
    return jnp.einsum(
        "qhgd,khd->hgqk", query_part, key_block, preferred_element_type=jnp.float32
    ) * DH ** (-0.5)


def prob_grad_of(grad_part, value_block):
    return jnp.einsum("qhgd,khd->hgqk", grad_part, value_block, preferred_element_type=jnp.float32)


def statistics(
    query_part, grad_part, pos_query, doc_query, key_blocks, value_blocks, pos_keys, doc_keys
):
    shape_stat = (query_part.shape[1], query_part.shape[2], query_part.shape[0])
    initial = (
        jnp.full(shape_stat, NEG, jnp.float32),
        jnp.zeros(shape_stat, jnp.float32),
        jnp.zeros(shape_stat, jnp.float32),
    )

    def one_tile(state_now, block_item):
        key_block, value_block, pos_key, doc_key = block_item
        visible_pairs = visible_of(pos_query, doc_query, pos_key, doc_key)

        def one_compute_tile(state_in):
            running_max, running_sum, running_dot = state_in
            scores = jnp.where(visible_pairs[None, None], scores_of(query_part, key_block), NEG)
            new_max = jnp.maximum(running_max, jnp.max(scores, axis=-1))
            expo_terms = jnp.where(
                visible_pairs[None, None], jnp.exp(scores - new_max[..., None]), 0.0
            )
            grad_prob = prob_grad_of(grad_part, value_block)
            rescale = jnp.exp(running_max - new_max)
            return (
                new_max,
                running_sum * rescale + jnp.sum(expo_terms, axis=-1),
                running_dot * rescale + jnp.sum(expo_terms * grad_prob, axis=-1),
            )

        def one_skip_tile(state_in):
            return state_in

        return (lax.cond(jnp.any(visible_pairs), one_compute_tile, one_skip_tile, state_now), None)

    (running_max, running_sum, running_dot), unused = lax.scan(
        one_tile, initial, (key_blocks, value_blocks, pos_keys, doc_keys)
    )
    return (running_max + jnp.log(running_sum), running_dot / running_sum)


def tile_weights(
    query_part, grad_part, key_block, value_block, visible_pairs, log_total, correction
):
    scores = scores_of(query_part, key_block)
    grad_prob = prob_grad_of(grad_part, value_block)
    weights = jnp.where(visible_pairs[None, None], jnp.exp(scores - log_total[..., None]), 0.0)
    grad_score = DH ** (-0.5) * weights * (grad_prob - correction[..., None])
    return (weights.astype(jnp.bfloat16), grad_score.astype(jnp.bfloat16))


def key_terms(query_part, grad_part, weights_low, grad_score, key_rows):
    key_grad = jnp.einsum(
        "hgqk,qhgd->khd", grad_score, query_part, preferred_element_type=jnp.float32
    )
    value_grad = jnp.einsum(
        "hgqk,qhgd->khd", weights_low, grad_part, preferred_element_type=jnp.float32
    )
    return jnp.concatenate(
        [key_grad.reshape(key_rows, -1), value_grad.reshape(key_rows, -1)], axis=1
    )


def per_device(queries, key_states, value_states, grad_output, doc_ids):
    group_size = lax.axis_size("ctx")
    device_index = lax.axis_index("ctx")
    local_rows = queries.shape[0]
    half_rows = local_rows // 2
    total_rows = local_rows * group_size
    kv_heads = key_states.shape[1] // DH
    block_count = total_rows // KEY_BLOCK
    term_width = 2 * kv_heads * DH
    all_keys, all_values = (
        lax.all_gather(key_states, "ctx", axis=0, tiled=True),
        lax.all_gather(value_states, "ctx", axis=0, tiled=True),
    )
    positions = storage_order(jnp.arange(total_rows, dtype=jnp.int32), group_size)
    documents = storage_order(doc_ids, group_size)
    my_positions = lax.dynamic_slice_in_dim(positions, device_index * local_rows, local_rows)
    my_documents = lax.dynamic_slice_in_dim(documents, device_index * local_rows, local_rows)
    keys_wide = all_keys.reshape(total_rows, kv_heads, DH)
    values_wide = all_values.reshape(total_rows, kv_heads, DH)
    key_blocks = keys_wide.reshape(block_count, KEY_BLOCK, kv_heads, DH)
    value_blocks = values_wide.reshape(block_count, KEY_BLOCK, kv_heads, DH)
    pos_keys = positions.reshape(block_count, KEY_BLOCK)
    doc_keys = documents.reshape(block_count, KEY_BLOCK)
    query_four = queries.reshape(local_rows, kv_heads, GROUP, DH)
    grad_four = grad_output.reshape(local_rows, kv_heads, GROUP, DH)
    halves = []
    for half_index in range(2):
        low_row = half_index * half_rows
        query_part = query_four[low_row : low_row + half_rows]
        grad_part = grad_four[low_row : low_row + half_rows]
        pos_query = my_positions[low_row : low_row + half_rows]
        doc_query = my_documents[low_row : low_row + half_rows]
        log_total, correction = statistics(
            query_part,
            grad_part,
            pos_query,
            doc_query,
            key_blocks,
            value_blocks,
            pos_keys,
            doc_keys,
        )
        halves.append((query_part, grad_part, pos_query, doc_query, log_total, correction))
    zero_query = jnp.zeros((half_rows, kv_heads, GROUP, DH), jnp.float32)
    query_grads = []
    term_total = jnp.zeros((total_rows, term_width), jnp.float32)
    for query_part, grad_part, pos_query, doc_query, log_total, correction in halves:

        def grad_tile(query_grad, block_item):
            key_block, value_block, pos_key, doc_key = block_item
            visible_pairs = visible_of(pos_query, doc_query, pos_key, doc_key)

            def grad_compute_tile(query_in):
                weights_low, grad_score = tile_weights(
                    query_part,
                    grad_part,
                    key_block,
                    value_block,
                    visible_pairs,
                    log_total,
                    correction,
                )
                query_out = query_in + jnp.einsum(
                    "hgqk,khd->qhgd", grad_score, key_block, preferred_element_type=jnp.float32
                )
                return (
                    query_out,
                    key_terms(query_part, grad_part, weights_low, grad_score, KEY_BLOCK),
                )

            def grad_skip_tile(query_in):
                return (query_in, jnp.zeros((KEY_BLOCK, term_width), jnp.float32))

            return lax.cond(jnp.any(visible_pairs), grad_compute_tile, grad_skip_tile, query_grad)

        query_grad, terms = lax.scan(
            grad_tile, zero_query, (key_blocks, value_blocks, pos_keys, doc_keys)
        )
        query_grads.append(query_grad)
        term_total = term_total + terms.reshape(total_rows, term_width)
    owned = lax.psum_scatter(
        term_total.astype(jnp.bfloat16), "ctx", scatter_dimension=0, tiled=True
    ).astype(jnp.float32)
    query_grad = jnp.concatenate(
        [piece.reshape(half_rows, -1) for piece in query_grads], axis=0
    ).astype(jnp.bfloat16)
    key_grad = owned[:, : kv_heads * DH].astype(jnp.bfloat16)
    value_grad = owned[:, kv_heads * DH :].astype(jnp.bfloat16)
    return (query_grad, key_grad, value_grad)


def solution(mesh):
    placed = (
        P(("dp", "ctx"), None),
        P(("dp", "ctx"), None),
        P(("dp", "ctx"), None),
        P(("dp", "ctx"), None),
        P("dp"),
    )
    return jax.shard_map(
        per_device,
        mesh=mesh,
        in_specs=placed,
        out_specs=(P(("dp", "ctx"), None), P(("dp", "ctx"), None), P(("dp", "ctx"), None)),
        check_vma=False,
    )
```

profile of v0, /device:TPU:23, one launch (start us, length us, event | category | flops | bytes accessed | tf_op | source)
XLA Modules:
  0.0 497.8 jit_solution(1126976502878645738)
XLA Ops:
  13.4 39.3 %all-gather.3.cloned.1.call-done = bf16[2048,512]{1,0:T(8,128)(2,1)} async-done(((bf16[128,512]{1,0:T(8,128)(2,1)}), bf16[2048,512]{1,0:T(8,128)(2,1)}) %all-gather.3.cloned.1.call-update) | async-done | bytes 2097168 | tf_op jit(solution)/shard_map/all_gather | solution.py:105
  60.2 32.4 %all-gather.5.cloned.1.call-done = bf16[2048,512]{1,0:T(8,128)(2,1)} async-done(((bf16[128,512]{1,0:T(8,128)(2,1)}), bf16[2048,512]{1,0:T(8,128)(2,1)}) %all-gather.5.cloned.1.call-update) | async-done | bytes 2097168 | tf_op jit(solution)/shard_map/all_gather | solution.py:106
  100.1 30.5 %while.58 = (s32[]{:T(128)}, f32[4,8,64]{2,1,0:T(8,128)S(1)}, f32[4,8,64]{2,1,0:T(8,128)S(1)}, f32[4,8,64]{2,1,0:T(8,128)S(1)}, s32[16,128]{1,0:T(8,128)S(1)}, /...) while((s32[]{:T(128)}, f32[4,8,64]{2,1,0:T(8,128)S(1)}, ...), condition=%wide.region_7.8_spmd, body=%wide.region_0.7_spmd.sunk | while | flops 136878080 | bytes 4641551 | solution.py:67
  130.6 78.8 %while.60 = (s32[]{:T(128)}, f32[4,8,64]{2,1,0:T(8,128)S(1)}, f32[4,8,64]{2,1,0:T(8,128)S(1)}, f32[4,8,64]{2,1,0:T(8,128)S(1)}, s32[16,128]{1,0:T(8,128)S(1)}, /...) while((s32[]{:T(128)}, f32[4,8,64]{2,1,0:T(8,128)S(1)}, ...), condition=%wide.region_20.21_spmd, body=%wide.region_13.20_spmd.sunk | while | flops 136878080 | bytes 4641551 | solution.py:67
  214.6 115.0 %while.61 = (s32[]{:T(128)}, f32[64,4,8,128]{3,0,2,1:T(8,128)}, f32[16,128,1024]{1,2,0:T(8,128)}, s32[16,128]{1,0:T(8,128)S(1)}, s32[64]{0:T(128)S(1)}, /*index=...) while((s32[]{:T(128)}, f32[64,4,8,128]{3,0,2,1:T(8,128)}, ...), condition=%wide.region_25.26_spmd, body=%wide.region_21.25_spmd.sunk | while | flops 338067456 | bytes 20354856 | solution.py:170
  218.4 5.3 %conditional.11 = (f32[64,4,8,128]{3,0,2,1:T(8,128)}, f32[1,128,1024]{1,2,0:T(8,128)S(1)}) conditional(s32[]{:T(128)} %convert_element_type.58, f32[64,4,8,128]{3,0,2,1:T(8,128)} %get-tuple-element.1223, (pred[64,128]{1,0:T(8,128)(4,1)S(1)}, bf16[16,128,4,128]{3,1,2,0:T(8,128)(2,1)}, s32[]{:T(128)}, bf16[64,4,8,128]{3,0,2,1:T(8,128)(2,1)S(1)}, ...), branch_computations={%region_23.23_spmd, %region_24.24_spmd} | conditional | flops 338034688 | bytes 19293768 | solution.py:168
  225.9 5.3 %conditional.11 = (f32[64,4,8,128]{3,0,2,1:T(8,128)}, f32[1,128,1024]{1,2,0:T(8,128)S(1)}) conditional(s32[]{:T(128)} %convert_element_type.58, f32[64,4,8,128]{3,0,2,1:T(8,128)} %get-tuple-element.1223, (pred[64,128]{1,0:T(8,128)(4,1)S(1)}, bf16[16,128,4,128]{3,1,2,0:T(8,128)(2,1)}, s32[]{:T(128)}, bf16[64,4,8,128]{3,0,2,1:T(8,128)(2,1)S(1)}, ...), branch_computations={%region_23.23_spmd, %region_24.24_spmd} | conditional | flops 338034688 | bytes 19293768 | solution.py:168
  233.4 5.3 %conditional.11 = (f32[64,4,8,128]{3,0,2,1:T(8,128)}, f32[1,128,1024]{1,2,0:T(8,128)S(1)}) conditional(s32[]{:T(128)} %convert_element_type.58, f32[64,4,8,128]{3,0,2,1:T(8,128)} %get-tuple-element.1223, (pred[64,128]{1,0:T(8,128)(4,1)S(1)}, bf16[16,128,4,128]{3,1,2,0:T(8,128)(2,1)}, s32[]{:T(128)}, bf16[64,4,8,128]{3,0,2,1:T(8,128)(2,1)S(1)}, ...), branch_computations={%region_23.23_spmd, %region_24.24_spmd} | conditional | flops 338034688 | bytes 19293768 | solution.py:168
  240.9 5.3 %conditional.11 = (f32[64,4,8,128]{3,0,2,1:T(8,128)}, f32[1,128,1024]{1,2,0:T(8,128)S(1)}) conditional(s32[]{:T(128)} %convert_element_type.58, f32[64,4,8,128]{3,0,2,1:T(8,128)} %get-tuple-element.1223, (pred[64,128]{1,0:T(8,128)(4,1)S(1)}, bf16[16,128,4,128]{3,1,2,0:T(8,128)(2,1)}, s32[]{:T(128)}, bf16[64,4,8,128]{3,0,2,1:T(8,128)(2,1)S(1)}, ...), branch_computations={%region_23.23_spmd, %region_24.24_spmd} | conditional | flops 338034688 | bytes 19293768 | solution.py:168
  248.4 5.3 %conditional.11 = (f32[64,4,8,128]{3,0,2,1:T(8,128)}, f32[1,128,1024]{1,2,0:T(8,128)S(1)}) conditional(s32[]{:T(128)} %convert_element_type.58, f32[64,4,8,128]{3,0,2,1:T(8,128)} %get-tuple-element.1223, (pred[64,128]{1,0:T(8,128)(4,1)S(1)}, bf16[16,128,4,128]{3,1,2,0:T(8,128)(2,1)}, s32[]{:T(128)}, bf16[64,4,8,128]{3,0,2,1:T(8,128)(2,1)S(1)}, ...), branch_computations={%region_23.23_spmd, %region_24.24_spmd} | conditional | flops 338034688 | bytes 19293768 | solution.py:168
  255.9 5.3 %conditional.11 = (f32[64,4,8,128]{3,0,2,1:T(8,128)}, f32[1,128,1024]{1,2,0:T(8,128)S(1)}) conditional(s32[]{:T(128)} %convert_element_type.58, f32[64,4,8,128]{3,0,2,1:T(8,128)} %get-tuple-element.1223, (pred[64,128]{1,0:T(8,128)(4,1)S(1)}, bf16[16,128,4,128]{3,1,2,0:T(8,128)(2,1)}, s32[]{:T(128)}, bf16[64,4,8,128]{3,0,2,1:T(8,128)(2,1)S(1)}, ...), branch_computations={%region_23.23_spmd, %region_24.24_spmd} | conditional | flops 338034688 | bytes 19293768 | solution.py:168
  263.4 5.3 %conditional.11 = (f32[64,4,8,128]{3,0,2,1:T(8,128)}, f32[1,128,1024]{1,2,0:T(8,128)S(1)}) conditional(s32[]{:T(128)} %convert_element_type.58, f32[64,4,8,128]{3,0,2,1:T(8,128)} %get-tuple-element.1223, (pred[64,128]{1,0:T(8,128)(4,1)S(1)}, bf16[16,128,4,128]{3,1,2,0:T(8,128)(2,1)}, s32[]{:T(128)}, bf16[64,4,8,128]{3,0,2,1:T(8,128)(2,1)S(1)}, ...), branch_computations={%region_23.23_spmd, %region_24.24_spmd} | conditional | flops 338034688 | bytes 19293768 | solution.py:168
  270.9 5.3 %conditional.11 = (f32[64,4,8,128]{3,0,2,1:T(8,128)}, f32[1,128,1024]{1,2,0:T(8,128)S(1)}) conditional(s32[]{:T(128)} %convert_element_type.58, f32[64,4,8,128]{3,0,2,1:T(8,128)} %get-tuple-element.1223, (pred[64,128]{1,0:T(8,128)(4,1)S(1)}, bf16[16,128,4,128]{3,1,2,0:T(8,128)(2,1)}, s32[]{:T(128)}, bf16[64,4,8,128]{3,0,2,1:T(8,128)(2,1)S(1)}, ...), branch_computations={%region_23.23_spmd, %region_24.24_spmd} | conditional | flops 338034688 | bytes 19293768 | solution.py:168
  278.5 5.3 %conditional.11 = (f32[64,4,8,128]{3,0,2,1:T(8,128)}, f32[1,128,1024]{1,2,0:T(8,128)S(1)}) conditional(s32[]{:T(128)} %convert_element_type.58, f32[64,4,8,128]{3,0,2,1:T(8,128)} %get-tuple-element.1223, (pred[64,128]{1,0:T(8,128)(4,1)S(1)}, bf16[16,128,4,128]{3,1,2,0:T(8,128)(2,1)}, s32[]{:T(128)}, bf16[64,4,8,128]{3,0,2,1:T(8,128)(2,1)S(1)}, ...), branch_computations={%region_23.23_spmd, %region_24.24_spmd} | conditional | flops 338034688 | bytes 19293768 | solution.py:168
  286.0 5.3 %conditional.11 = (f32[64,4,8,128]{3,0,2,1:T(8,128)}, f32[1,128,1024]{1,2,0:T(8,128)S(1)}) conditional(s32[]{:T(128)} %convert_element_type.58, f32[64,4,8,128]{3,0,2,1:T(8,128)} %get-tuple-element.1223, (pred[64,128]{1,0:T(8,128)(4,1)S(1)}, bf16[16,128,4,128]{3,1,2,0:T(8,128)(2,1)}, s32[]{:T(128)}, bf16[64,4,8,128]{3,0,2,1:T(8,128)(2,1)S(1)}, ...), branch_computations={%region_23.23_spmd, %region_24.24_spmd} | conditional | flops 338034688 | bytes 19293768 | solution.py:168
  293.5 5.3 %conditional.11 = (f32[64,4,8,128]{3,0,2,1:T(8,128)}, f32[1,128,1024]{1,2,0:T(8,128)S(1)}) conditional(s32[]{:T(128)} %convert_element_type.58, f32[64,4,8,128]{3,0,2,1:T(8,128)} %get-tuple-element.1223, (pred[64,128]{1,0:T(8,128)(4,1)S(1)}, bf16[16,128,4,128]{3,1,2,0:T(8,128)(2,1)}, s32[]{:T(128)}, bf16[64,4,8,128]{3,0,2,1:T(8,128)(2,1)S(1)}, ...), branch_computations={%region_23.23_spmd, %region_24.24_spmd} | conditional | flops 338034688 | bytes 19293768 | solution.py:168
  301.0 5.3 %conditional.11 = (f32[64,4,8,128]{3,0,2,1:T(8,128)}, f32[1,128,1024]{1,2,0:T(8,128)S(1)}) conditional(s32[]{:T(128)} %convert_element_type.58, f32[64,4,8,128]{3,0,2,1:T(8,128)} %get-tuple-element.1223, (pred[64,128]{1,0:T(8,128)(4,1)S(1)}, bf16[16,128,4,128]{3,1,2,0:T(8,128)(2,1)}, s32[]{:T(128)}, bf16[64,4,8,128]{3,0,2,1:T(8,128)(2,1)S(1)}, ...), branch_computations={%region_23.23_spmd, %region_24.24_spmd} | conditional | flops 338034688 | bytes 19293768 | solution.py:168
  308.5 5.3 %conditional.11 = (f32[64,4,8,128]{3,0,2,1:T(8,128)}, f32[1,128,1024]{1,2,0:T(8,128)S(1)}) conditional(s32[]{:T(128)} %convert_element_type.58, f32[64,4,8,128]{3,0,2,1:T(8,128)} %get-tuple-element.1223, (pred[64,128]{1,0:T(8,128)(4,1)S(1)}, bf16[16,128,4,128]{3,1,2,0:T(8,128)(2,1)}, s32[]{:T(128)}, bf16[64,4,8,128]{3,0,2,1:T(8,128)(2,1)S(1)}, ...), branch_computations={%region_23.23_spmd, %region_24.24_spmd} | conditional | flops 338034688 | bytes 19293768 | solution.py:168
  316.0 5.3 %conditional.11 = (f32[64,4,8,128]{3,0,2,1:T(8,128)}, f32[1,128,1024]{1,2,0:T(8,128)S(1)}) conditional(s32[]{:T(128)} %convert_element_type.58, f32[64,4,8,128]{3,0,2,1:T(8,128)} %get-tuple-element.1223, (pred[64,128]{1,0:T(8,128)(4,1)S(1)}, bf16[16,128,4,128]{3,1,2,0:T(8,128)(2,1)}, s32[]{:T(128)}, bf16[64,4,8,128]{3,0,2,1:T(8,128)(2,1)S(1)}, ...), branch_computations={%region_23.23_spmd, %region_24.24_spmd} | conditional | flops 338034688 | bytes 19293768 | solution.py:168
  323.6 5.3 %conditional.11 = (f32[64,4,8,128]{3,0,2,1:T(8,128)}, f32[1,128,1024]{1,2,0:T(8,128)S(1)}) conditional(s32[]{:T(128)} %convert_element_type.58, f32[64,4,8,128]{3,0,2,1:T(8,128)} %get-tuple-element.1223, (pred[64,128]{1,0:T(8,128)(4,1)S(1)}, bf16[16,128,4,128]{3,1,2,0:T(8,128)(2,1)}, s32[]{:T(128)}, bf16[64,4,8,128]{3,0,2,1:T(8,128)(2,1)S(1)}, ...), branch_computations={%region_23.23_spmd, %region_24.24_spmd} | conditional | flops 338034688 | bytes 19293768 | solution.py:168
  333.9 45.8 %while.59 = (s32[]{:T(128)}, f32[64,4,8,128]{3,0,2,1:T(8,128)S(1)}, f32[16,128,1024]{1,2,0:T(8,128)}, s32[16,128]{1,0:T(8,128)S(1)}, s32[64]{0:T(128)S(1)}, /*in...) while((s32[]{:T(128)}, f32[64,4,8,128]{3,0,2,1:T(8,128)S(1)}, ...), condition=%wide.region_12.13_spmd, body=%wide.region_8.12_spmd.sunk | while | flops 338067456 | bytes 11966191 | solution.py:170
  379.7 8.6 %add_convert_fusion = bf16[16,128,1024]{1,2,0:T(8,128)(2,1)} fusion(f32[16,128,1024]{1,2,0:T(8,128)} %get-tuple-element.597, f32[16,128,1024]{1,2,0:T(8,128)} %get-tuple-element.598), kind=kLoop, calls=%fused_computation.102 | loop fusion | flops 4194304 | bytes 20971520 | tf_op jit(solution)/shard_map/convert_element_type | solution.py:176
  388.3 6.4 %copy.33 = bf16[16,128,1024]{2,1,0:T(8,128)(2,1)} copy(bf16[16,128,1024]{1,2,0:T(8,128)(2,1)} %add_convert_fusion) | data formatting | bytes 8388608 | tf_op jit(solution)/shard_map/convert_element_type | solution.py:176
  398.3 91.3 %reduce-scatter.2.cloned.1.call-done = bf16[128,1024]{1,0:T(8,128)(2,1)} async-done(((bf16[2048,1024]{1,0:T(8,128)(2,1)}), bf16[128,1024]{1,0:T(8,128)(2,1)}) %reduce-scatter.2.cloned.1.call-update) | async-done | bytes 262160 | tf_op jit(solution)/shard_map/reduce_scatter | solution.py:175
  (548 shorter events, 334.2 us)
Async XLA Ops:
  7.2 45.6 %all-gather.3.cloned.1.call-start = ((), (), s32[]{:S(2)}) async-start(), calls=%async_computation.1 | async-start | bytes 2228224 | tf_op jit(solution)/shard_map/all_gather | solution.py:105
  7.9 84.7 %all-gather.5.cloned.1.call-start = ((), (), s32[]{:S(2)}) async-start(), calls=%async_computation.2 | async-start | bytes 2228224 | tf_op jit(solution)/shard_map/all_gather | solution.py:106
  8.6 481.0 %reduce-scatter.2.cloned.1.call-start = ((), (), s32[]{:S(2)}) async-start(), calls=%async_computation.3 | async-start | bytes 4456448 | tf_op jit(solution)/shard_map/reduce_scatter | solution.py:175
  11.4 1.2 copy-start.3
  219.7 1.7 copy-start
  227.2 1.7 copy-start
  230.2 1.0 copy-start.1
  234.7 1.7 copy-start
  237.7 1.0 copy-start.1
  242.2 1.7 copy-start
  249.7 1.7 copy-start
  257.2 1.7 copy-start
  260.2 1.0 copy-start.1
  264.7 1.8 copy-start
  267.7 1.0 copy-start.1
  272.3 1.7 copy-start
  279.8 1.7 copy-start
  287.3 1.7 copy-start
  294.8 1.7 copy-start
  302.3 1.7 copy-start
  309.8 1.7 copy-start
  317.4 1.7 copy-start
  324.9 1.7 copy-start
  394.7 1.2 copy-start.2
  (11 other events, 10.7 us)
Sparse Core Ops, SparseCore 0:
  9.8 42.8 all-gather.2
  54.6 38.0 all-gather.4
  394.8 94.7 reduce-scatter.1
where the time goes:
time: 504 us; the launch traced here: 498 us
  waiting for transfers between devices  164 us (33%)
  matrix products  128 us (25%)
  local copies, waits for them, and re-layouts  76 us (15%)
  other arithmetic  69.5 us (14%)
  loops' own time  45.3 us (9%)
  between operations  14 us (3%)
    reduce_scatter x1, waiting for transfers between devices, per_device(): lax.psum_scatter(term_total.astype(jnp.bfloat16), 'ctx', scatter_dimensio...  91.3 us
    dot_general x34, matrix products, prob_grad_of(): jnp.einsum('qhgd,khd->hgqk', grad_part, value_block, preferred_element_ty...  49.9 us
    dot_general x34, matrix products, scores_of(): jnp.einsum('qhgd,khd->hgqk', query_part, key_block, preferred_element_typ...  46.4 us
    all_gather x1, waiting for transfers between devices, per_device(): lax.all_gather(key_states, 'ctx', axis=0, tiled=True)  39.3 us
    all_gather x1, waiting for transfers between devices, per_device(): lax.all_gather(value_states, 'ctx', axis=0, tiled=True)  32.4 us
    dynamic_update_slice x32, local copies, waits for them, and re-layouts, per_device(): lax.scan(grad_tile, zero_query, (key_blocks, value_blocks, pos_keys, doc_...  27 us
    reduce_or x32, other arithmetic, one_tile(): jnp.any(visible_pairs)  23.9 us
    reduce_or x32, other arithmetic, grad_tile(): jnp.any(visible_pairs)  23.5 us
  transfers between devices with their start and end apart: 3, of which 3 were waited for; matrix products, arithmetic and copies ran while one was open for 3% of the time, Pallas kernels for 0%

commit v1 on v0

v1 whole, which is shorter than its diff:
```python
import functools

import jax
import jax.numpy as jnp
from jax import lax
from jax.experimental import pallas as pl
from jax.experimental.pallas import tpu as pltpu
from jax.sharding import PartitionSpec as P

DH = 128
GROUP = 8
SCALE = DH ** (-0.5)
LOG2E = 1.4426950408889634
NEG = -1e30
LOW = -1e29
NZ = 8
BLK = 128
NB = 16
LANES = GROUP * BLK
VMEM = 56 * 1024 * 1024

NT = (((1,), (1,)), ((), ()))
NN = (((1,), (0,)), ((), ()))
TN = (((0,), (0,)), ((), ()))


def dot(a, b, dims):
    return lax.dot_general(a, b, dims, preferred_element_type=jnp.float32)


def attention_kernel(
    place, doc_ref, q_ref, do_ref, qd_ref,
    c0, u1, u2, u3, d1, d2, d3, k4, v4,
    dq_own, dq_par, t0, tu1, tu2, tu3, td1, td2, td3, t4,
    qv, dov, kv, qst, dst, acc, dqt, pbuf, gbuf, mbuf, sem,
):
    core, z = place[0], place[1]
    copies = []

    def copy(src, dst):
        copies.append(pltpu.make_async_copy(src, dst, sem.at[len(copies)]))
        copies[-1].start()

    col = pl.multiple_of(core * 2048, 2048)
    copy(q_ref.at[:, pl.ds(col, 2048)], qv.at[0])
    copy(do_ref.at[:, pl.ds(col, 2048)], dov.at[0])
    copy(qd_ref.at[:, pl.ds(0, 2048)], qv.at[1])
    copy(qd_ref.at[:, pl.ds(2048, 2048)], dov.at[1])

    def chip(offset):
        return lax.rem(z + offset + NZ, NZ)

    for chunk, offset in ((c0, 0), (u1, -1), (u2, -2), (u3, -3), (d1, 1), (d2, 2), (d3, 3)):
        s = chip(offset)
        copy(chunk.at[pl.ds(0, BLK)], kv.at[s])
        copy(chunk.at[pl.ds(BLK, BLK)], kv.at[NB - 1 - s])
    far = chip(4)
    for part, low in ((k4, 0), (v4, 256)):
        copy(part.at[pl.ds(0, BLK)], kv.at[far, :, pl.ds(low, 256)])
        copy(part.at[pl.ds(BLK, BLK)], kv.at[NB - 1 - far, :, pl.ds(low, 256)])
    acc[...] = jnp.zeros_like(acc)

    doc = doc_ref[...]
    starts = [jnp.sum((doc < d).astype(jnp.float32)).astype(jnp.int32) for d in (1, 2, 3)]
    for one in copies:
        one.wait()
    for x in range(2):
        for g in range(2):
            for h in range(GROUP):
                cols = slice((g * GROUP + h) * DH, (g * GROUP + h + 1) * DH)
                for half in range(2):
                    rows = slice(h * BLK + half * 64, h * BLK + half * 64 + 64)
                    qst[2 * x + g, rows, :] = qv[half, x * 64:x * 64 + 64, cols]
                    dst[2 * x + g, rows, :] = dov[half, x * 64:x * 64 + 64, cols]

    def one_set(xg, unused):
        x, g = lax.div(xg, 2), lax.rem(xg, 2)
        qb = jnp.where(x == 0, z, NB - 1 - z)
        flip_q = jnp.where(qb < NZ, core, 1 - core)
        lane = lax.broadcasted_iota(jnp.int32, (1, BLK), 1)
        rot = jnp.where(flip_q == 1, lax.rem(lane + 64, BLK), lane)
        doc_row = doc_ref[pl.ds(qb, 1), :]
        doc_row = jnp.where(flip_q == 1, pltpu.roll(doc_row, 64, 1), doc_row)
        pos_q = qb * BLK + rot
        start_q = jnp.where(
            doc_row == 0, 0,
            jnp.where(doc_row == 1, starts[0], jnp.where(doc_row == 2, starts[1], starts[2])),
        )
        low_block = lax.div(jnp.min(start_q), BLK)
        kcol = pl.multiple_of(g * DH, DH)
        vcol = pl.multiple_of(256 + g * DH, DH)

        def first(b, state):
            m, l, d = state
            flip_k = jnp.where(b < NZ, core, 1 - core)
            row = lax.broadcasted_iota(jnp.int32, (BLK, 1), 0)
            pos_k = b * BLK + jnp.where(flip_k == 1, lax.rem(row + 64, BLK), row)
            bias = jnp.where((pos_k <= pos_q) & (pos_k >= start_q), 0.0, NEG)
            bias = jnp.concatenate([bias] * GROUP, axis=1)
            s = dot(kv[b, :, pl.ds(kcol, DH)], qst[xg], NT) * (SCALE * LOG2E) + bias
            new = jnp.maximum(m, jnp.max(s, axis=0, keepdims=True))
            p = jnp.exp2(s - new)
            grad = dot(kv[b, :, pl.ds(vcol, DH)], dst[xg], NT)
            i = b - low_block
            pbuf[i] = p
            gbuf[i] = grad
            mbuf[i] = new
            alpha = jnp.exp2(m - new)
            return (
                new,
                l * alpha + jnp.sum(p, axis=0, keepdims=True),
                d * alpha + jnp.sum(p * grad, axis=0, keepdims=True),
            )

        zero = jnp.zeros((1, LANES), jnp.float32)
        m, l, d = lax.fori_loop(low_block, qb + 1, first, (zero + LOW, zero, zero))
        inv = 1.0 / l
        corr = d * inv
        dqt[...] = jnp.zeros_like(dqt)

        def second(b, unused):
            i = b - low_block
            w = pbuf[i] * (jnp.exp2(mbuf[i] - m) * inv)
            ds = (w * (gbuf[i] - corr)).astype(jnp.bfloat16)
            acc[b, :, pl.ds(kcol, DH)] += dot(ds, qst[xg], NN)
            acc[b, :, pl.ds(vcol, DH)] += dot(w.astype(jnp.bfloat16), dst[xg], NN)
            dqt[...] += dot(kv[b, :, pl.ds(kcol, DH)], ds, TN)
            return 0

        lax.fori_loop(low_block, qb + 1, second, 0)
        rows = pl.multiple_of(x * 64, 64)
        for h in range(GROUP):
            out = jnp.transpose(dqt[:, h * BLK:(h + 1) * BLK] * SCALE).astype(jnp.bfloat16)
            ocol = pl.multiple_of((g * GROUP + h) * DH, DH)
            dq_own[pl.ds(rows, 64), pl.ds(ocol, DH)] = out[:64]
            dq_par[pl.ds(rows, 64), pl.ds(ocol, DH)] = out[64:]
        return 0

    lax.fori_loop(0, 4, one_set, 0)
    for out, offset in (
        (t0, 0), (tu1, 1), (tu2, 2), (tu3, 3), (td1, -1), (td2, -2), (td3, -3), (t4, 4)
    ):
        s = chip(offset)
        for part, b in ((0, s), (1, NB - 1 - s)):
            rows = slice(part * BLK, part * BLK + BLK)
            out[rows, :256] = (acc[b, :, :256] * SCALE).astype(jnp.bfloat16)
            out[rows, 256:] = acc[b, :, 256:].astype(jnp.bfloat16)


def attention(place, doc, queries, grad_output, qd, chunks):
    half = jax.ShapeDtypeStruct((BLK, 2048), jnp.bfloat16)
    term = jax.ShapeDtypeStruct((256, 512), jnp.bfloat16)
    any_space = pl.BlockSpec(memory_space=pl.ANY)
    vmem = pl.BlockSpec(memory_space=pltpu.VMEM)
    return pl.pallas_call(
        attention_kernel,
        out_shape=(half, half) + (term,) * 8,
        in_specs=[pl.BlockSpec(memory_space=pltpu.SMEM), vmem] + [any_space] * 12,
        out_specs=(vmem,) * 10,
        scratch_shapes=[
            pltpu.VMEM((2, BLK, 2048), jnp.bfloat16),
            pltpu.VMEM((2, BLK, 2048), jnp.bfloat16),
            pltpu.VMEM((NB, BLK, 512), jnp.bfloat16),
            pltpu.VMEM((4, LANES, DH), jnp.bfloat16),
            pltpu.VMEM((4, LANES, DH), jnp.bfloat16),
            pltpu.VMEM((NB, BLK, 512), jnp.float32),
            pltpu.VMEM((DH, LANES), jnp.float32),
            pltpu.VMEM((NB // 2 + 1, BLK, LANES), jnp.float32),
            pltpu.VMEM((NB // 2 + 1, BLK, LANES), jnp.float32),
            pltpu.VMEM((NB // 2 + 1, 1, LANES), jnp.float32),
            pltpu.SemaphoreType.DMA((22,)),
        ],
        compiler_params=pltpu.CompilerParams(vmem_limit_bytes=VMEM),
        cost_estimate=pl.CostEstimate(flops=10**10, bytes_accessed=10**7, transcendentals=10**7),
    )(place, doc, queries, grad_output, qd, *chunks)


def ring(step):
    return [(2 * z + c, 2 * ((z + step) % NZ) + c) for z in range(NZ) for c in range(2)]


SWAP = [(i, i ^ 1) for i in range(2 * NZ)]


def send(x, pairs):
    return lax.ppermute(x, "ctx", pairs)


def half_of(x, index):
    width = x.shape[1] // 2
    return lax.dynamic_slice_in_dim(x, index * width, width, 1)


def join(mine, other, core):
    return jnp.where(
        core == 0,
        jnp.concatenate([mine, other], axis=1),
        jnp.concatenate([other, mine], axis=1),
    )


def per_device(queries, key_states, value_states, grad_output, doc_ids):
    index = lax.axis_index("ctx")
    core, z = index % 2, index // 2
    place = jnp.stack([core, z]).astype(jnp.int32)
    doc = doc_ids.reshape(NB, BLK)

    mine = jnp.concatenate([half_of(key_states, core), half_of(value_states, core)], axis=1)
    other = jnp.concatenate([half_of(key_states, 1 - core), half_of(value_states, 1 - core)], axis=1)
    got = send(other, SWAP)
    qd = send(
        jnp.concatenate([half_of(queries, 1 - core), half_of(grad_output, 1 - core)], axis=1), SWAP
    )
    own = jnp.concatenate([mine[:64], got[:64], mine[64:], got[64:]], axis=0)
    up = down = own
    ups, downs = [], []
    for _ in range(3):
        up, down = send(up, ring(1)), send(down, ring(-1))
        ups.append(up)
        downs.append(down)
    far_k, far_v = send(up[:, :256], ring(1)), send(down[:, 256:], ring(-1))

    dq_own, dq_par, t0, tu1, tu2, tu3, td1, td2, td3, t4 = attention(
        place, doc, queries, grad_output, qd, [own, *ups, *downs, far_k, far_v]
    )
    dq_got = send(dq_par, SWAP)

    def add(a, b):
        return (a.astype(jnp.float32) + b.astype(jnp.float32)).astype(jnp.bfloat16)

    up, down = send(t4[:, :256], ring(1)), send(t4[:, 256:], ring(-1))
    up = jnp.concatenate([add(tu3[:, :256], up), tu3[:, 256:]], axis=1)
    down = jnp.concatenate([td3[:, :256], add(td3[:, 256:], down)], axis=1)
    up, down = send(up, ring(1)), send(down, ring(-1))
    up, down = send(add(tu2, up), ring(1)), send(add(td2, down), ring(-1))
    up, down = send(add(tu1, up), ring(1)), send(add(td1, down), ring(-1))
    total = (
        t0.astype(jnp.float32) + up.astype(jnp.float32) + down.astype(jnp.float32)
    ).astype(jnp.bfloat16)
    keep = jnp.concatenate([total[:64], total[128:192]], axis=0)
    away = jnp.concatenate([total[64:128], total[192:]], axis=0)
    back = send(away, SWAP)
    query_grad = join(dq_own, dq_got, core)
    key_grad = join(keep[:, :256], back[:, :256], core)
    value_grad = join(keep[:, 256:], back[:, 256:], core)
    return (query_grad, key_grad, value_grad)


def solution(mesh):
    rows = P(("dp", "ctx"), None)
    return jax.shard_map(
        per_device,
        mesh=mesh,
        in_specs=(rows, rows, rows, rows, P("dp")),
        out_specs=(rows, rows, rows),
        check_vma=False,
    )
```

time: 504 us -> 112 us (0.22)
  the two profiles are of different devices: /device:TPU:23 before, /device:TPU:25 now
where the time goes in v1:
time: 112 us; the launch traced here: 113 us
  starting transfers between devices  60.6 us (54%)
  waiting for transfers between devices  28.8 us (26%)
  Pallas kernels  12.9 us (12%)
  local copies, waits for them, and re-layouts  6.22 us (6%)
  other arithmetic  3.86 us (3%)
    ppermute x20, starting transfers between devices, send(): return lax.ppermute(x, 'ctx', pairs)  60.6 us
    ppermute x20, waiting for transfers between devices, send(): return lax.ppermute(x, 'ctx', pairs)  28.8 us
    pallas_call x1, Pallas kernels, attention(): pl.pallas_call(attention_kernel, out_shape=(half, half) + (term,) * 8, in...  12.9 us
    select_n x3, other arithmetic, join(): jnp.where(core == 0, jnp.concatenate([mine, other], axis=1), jnp.concaten...  2.59 us
    dynamic_slice x2, local copies, waits for them, and re-layouts, half_of(): return lax.dynamic_slice_in_dim(x, index * width, width, 1)  2.26 us
  transfers between devices with their start and end apart: 20, of which 10 were waited for; matrix products, arithmetic and copies ran while one was open for 5% of the time, Pallas kernels for 0%

profile of v1, /device:TPU:25, one launch (start us, length us, event | category | flops | bytes accessed | tf_op | source)
XLA Modules:
  0.0 113.4 jit_solution(9750197201850636320)
XLA Ops:
  2.4 1.3 %constant_dynamic-slice_fusion.4 = (bf16[128,2048]{1,0:T(8,128)(2,1)S(1)}, bf16[128,2048]{1,0:T(8,128)(2,1)S(1)}) fusion(bf16[128,4096]{1,0:T(8,128)(2,1)} %do_ref.1, s32[]{:T(128)S(6)} %select_n.46, bf16[128,4096]{1,0:T(8,128)(2,1)} %q_ref.1), kind=kLoop, calls=%fused_computation.34 | loop fusion | bytes 2097156 | tf_op jit(solution)/shard_map/dynamic_slice | solution.py:191
  4.0 5.7 %collective-permute-start.5 = (bf16[256,512]{1,0:T(8,128)(2,1)S(1)}, bf16[256,512]{1,0:T(8,128)(2,1)S(1)}, u32[]{:S(2)}, u32[]{:S(2)}) collective-permute-start(bf16[256,512]{1,0:T(8,128)(2,1)S(1)} %fusion.5.c0), channel_id=1, source_target_pairs={{0,14},{1,15},{2,0},{3,1},{4,2},{5,3},{6,4},{7,5},{8,6},{9,7},{10,... | collective-permute-start | bytes 786440 | tf_op jit(solution)/shard_map/ppermute | solution.py:186
  9.6 5.2 %collective-permute-done.5.d1 = bf16[256,512]{1,0:T(8,128)(2,1)S(1)} collective-permute-done((bf16[256,512]{1,0:T(8,128)(2,1)S(1)}, bf16[256,512]{1,0:T(8,128)(2,1)S(1)}, u32[]{:S(2)}, u32[]{:S(2)}) %collective-permute-start.5) | collective-permute-done | bytes 262176 | tf_op jit(solution)/shard_map/ppermute | solution.py:186
  14.8 3.4 %collective-permute-start.6 = (bf16[256,512]{1,0:T(8,128)(2,1)S(1)}, bf16[256,512]{1,0:T(8,128)(2,1)S(1)}, u32[]{:S(2)}, u32[]{:S(2)}) collective-permute-start(bf16[256,512]{1,0:T(8,128)(2,1)S(1)} %collective-permute-done.5.d1), channel_id=1, source_target_pairs={{0,14},{1,15},{2,0},{3,1},{4,2},{5,3},{6,4},{7,5},{8,6},{9,7},{10,... | collective-permute-start | bytes 786440 | tf_op jit(solution)/shard_map/ppermute | solution.py:186
  18.2 4.3 %collective-permute-done.6.d2 = bf16[256,512]{1,0:T(8,128)(2,1)S(1)} collective-permute-done((bf16[256,512]{1,0:T(8,128)(2,1)S(1)}, bf16[256,512]{1,0:T(8,128)(2,1)S(1)}, u32[]{:S(2)}, u32[]{:S(2)}) %collective-permute-start.6) | collective-permute-done | bytes 262176 | tf_op jit(solution)/shard_map/ppermute | solution.py:186
  22.5 3.4 %collective-permute-start.7 = (bf16[256,512]{1,0:T(8,128)(2,1)S(1)}, bf16[256,512]{1,0:T(8,128)(2,1)S(1)}, u32[]{:S(2)}, u32[]{:S(2)}) collective-permute-start(bf16[256,512]{1,0:T(8,128)(2,1)S(1)} %collective-permute-done.6.d2), channel_id=1, source_target_pairs={{0,14},{1,15},{2,0},{3,1},{4,2},{5,3},{6,4},{7,5},{8,6},{9,7},{10,... | collective-permute-start | bytes 786440 | tf_op jit(solution)/shard_map/ppermute | solution.py:186
  26.0 3.2 %collective-permute-done.7.d3 = bf16[256,512]{1,0:T(8,128)(2,1)S(1)} collective-permute-done((bf16[256,512]{1,0:T(8,128)(2,1)S(1)}, bf16[256,512]{1,0:T(8,128)(2,1)S(1)}, u32[]{:S(2)}, u32[]{:S(2)}) %collective-permute-start.7) | collective-permute-done | bytes 262176 | tf_op jit(solution)/shard_map/ppermute | solution.py:186
  29.2 3.5 %collective-permute-start.9 = (bf16[256,256]{1,0:T(8,128)(2,1)S(1)}, bf16[256,256]{1,0:T(8,128)(2,1)S(1)}, u32[]{:S(2)}, u32[]{:S(2)}) collective-permute-start(bf16[256,256]{1,0:T(8,128)(2,1)S(1)} %slice.85), channel_id=1, source_target_pairs={{0,14},{1,15},{2,0},{3,1},{4,2},{5,3},{6,4},{7,5},{8,6},{9,7},{10,... | collective-permute-start | bytes 393224 | tf_op jit(solution)/shard_map/ppermute | solution.py:186
  33.6 1.2 %collective-permute-done.9.v4 = bf16[256,256]{1,0:T(8,128)(2,1)S(1)} collective-permute-done((bf16[256,256]{1,0:T(8,128)(2,1)S(1)}, bf16[256,256]{1,0:T(8,128)(2,1)S(1)}, u32[]{:S(2)}, u32[]{:S(2)}) %collective-permute-start.9) | collective-permute-done | bytes 131104 | tf_op jit(solution)/shard_map/ppermute | solution.py:186
  34.7 3.3 %collective-permute-done.8.k4 = bf16[256,256]{1,0:T(8,128)(2,1)} collective-permute-done((bf16[256,256]{1,0:T(8,128)(2,1)S(1)}, bf16[256,256]{1,0:T(8,128)(2,1)}, u32[]{:S(2)}, u32[]{:S(2)}) %collective-permute-start.8) | collective-permute-done | bytes 131104 | tf_op jit(solution)/shard_map/ppermute | solution.py:186
  39.0 12.9 %shard_map.76 = (bf16[128,2048]{1,0:T(8,128)(2,1)}, bf16[128,2048]{1,0:T(8,128)(2,1)}, bf16[256,512]{1,0:T(8,128)(2,1)}, bf16[256,512]{1,0:T(8,128)(2,1)}, bf16[...) custom-call(s32[2]{0:T(128)} %pad_add_fusion.place, ...), custom_call_target="tpu_custom_call" | custom-call | flops 10000000000 | bytes 10000000 | tf_op jit(solution)/shard_map/pallas_call | solution.py:155
  51.9 1.0 fusion.9
  52.9 15.8 %collective-permute-start.15 = (bf16[256,256]{1,0:T(8,128)(2,1)S(1)}, bf16[256,256]{1,0:T(8,128)(2,1)S(1)}, u32[]{:S(2)}, u32[]{:S(2)}) collective-permute-start(bf16[256,256]{1,0:T(8,128)(2,1)S(1)} %get-tuple-element.28), channel_id=1, source_target_pairs={{0,14},{1,15},{2,0},{3,1},{4,2},{5,3},{6,4},{7,5},{8,6},{9,7},{10,... | collective-permute-start | bytes 393224 | tf_op jit(solution)/shard_map/ppermute | solution.py:186
  70.8 3.1 %collective-permute-start.16 = (bf16[256,512]{1,0:T(8,128)(2,1)S(1)}, bf16[256,512]{1,0:T(8,128)(2,1)S(1)}, u32[]{:S(2)}, u32[]{:S(2)}) collective-permute-start(bf16[256,512]{1,0:T(8,128)(2,1)S(1)} %pad_maximum_fusion.2), channel_id=1, source_target_pairs={{0,14},{1,15},{2,0},{3,1},{4,2},{5,3},{6,4},{7,5},{8,6},{9,7},{10,... | collective-permute-start | bytes 786440 | tf_op jit(solution)/shard_map/ppermute | solution.py:186
  74.0 1.8 %collective-permute-done.11 = bf16[256,256]{1,0:T(8,128)(2,1)S(1)} collective-permute-done((bf16[256,256]{1,0:T(8,128)(2,1)S(1)}, bf16[256,256]{1,0:T(8,128)(2,1)S(1)}, u32[]{:S(2)}, u32[]{:S(2)}) %collective-permute-start.11) | collective-permute-done | bytes 131104 | tf_op jit(solution)/shard_map/ppermute | solution.py:186
  76.1 2.2 %collective-permute-done.16 = bf16[256,512]{1,0:T(8,128)(2,1)S(1)} collective-permute-done((bf16[256,512]{1,0:T(8,128)(2,1)S(1)}, bf16[256,512]{1,0:T(8,128)(2,1)S(1)}, u32[]{:S(2)}, u32[]{:S(2)}) %collective-permute-start.16) | collective-permute-done | bytes 262176 | tf_op jit(solution)/shard_map/ppermute | solution.py:186
  78.3 3.2 %collective-permute-start.17 = (bf16[256,512]{1,0:T(8,128)(2,1)S(1)}, bf16[256,512]{1,0:T(8,128)(2,1)S(1)}, u32[]{:S(2)}, u32[]{:S(2)}) collective-permute-start(bf16[256,512]{1,0:T(8,128)(2,1)S(1)} %add_convert_fusion.2), channel_id=1, source_target_pairs={{0,14},{1,15},{2,0},{3,1},{4,2},{5,3},{6,4},{7,5},{8,6},{9,7},{10,... | collective-permute-start | bytes 786440 | tf_op jit(solution)/shard_map/ppermute | solution.py:186
  81.5 2.1 %collective-permute-done.12 = bf16[256,512]{1,0:T(8,128)(2,1)S(1)} collective-permute-done((bf16[256,512]{1,0:T(8,128)(2,1)S(1)}, bf16[256,512]{1,0:T(8,128)(2,1)S(1)}, u32[]{:S(2)}, u32[]{:S(2)}) %collective-permute-start.12) | collective-permute-done | bytes 262176 | tf_op jit(solution)/shard_map/ppermute | solution.py:186
  83.8 3.3 %collective-permute-done.17 = bf16[256,512]{1,0:T(8,128)(2,1)S(1)} collective-permute-done((bf16[256,512]{1,0:T(8,128)(2,1)S(1)}, bf16[256,512]{1,0:T(8,128)(2,1)S(1)}, u32[]{:S(2)}, u32[]{:S(2)}) %collective-permute-start.17) | collective-permute-done | bytes 262176 | tf_op jit(solution)/shard_map/ppermute | solution.py:186
  87.2 3.2 %collective-permute-start.18 = (bf16[256,512]{1,0:T(8,128)(2,1)S(1)}, bf16[256,512]{1,0:T(8,128)(2,1)S(1)}, u32[]{:S(2)}, u32[]{:S(2)}) collective-permute-start(bf16[256,512]{1,0:T(8,128)(2,1)S(1)} %add_convert_fusion.1), channel_id=1, source_target_pairs={{0,14},{1,15},{2,0},{3,1},{4,2},{5,3},{6,4},{7,5},{8,6},{9,7},{10,... | collective-permute-start | bytes 786440 | tf_op jit(solution)/shard_map/ppermute | solution.py:186
  90.4 2.3 %collective-permute-done.13 = bf16[256,512]{1,0:T(8,128)(2,1)S(1)} collective-permute-done((bf16[256,512]{1,0:T(8,128)(2,1)S(1)}, bf16[256,512]{1,0:T(8,128)(2,1)S(1)}, u32[]{:S(2)}, u32[]{:S(2)}) %collective-permute-start.13) | collective-permute-done | bytes 262176 | tf_op jit(solution)/shard_map/ppermute | solution.py:186
  92.8 10.2 %collective-permute-start.10 = (bf16[128,2048]{1,0:T(8,128)(2,1)S(1)}, bf16[128,2048]{1,0:T(8,128)(2,1)S(1)}, u32[]{:S(2)}, u32[]{:S(2)}) collective-permute-start(bf16[128,2048]{1,0:T(8,128)(2,1)S(1)} %copy-done.12), channel_id=1, source_target_pairs={{0,1},{1,0},{2,3},{3,2},{4,5},{5,4},{6,7},{7,6},{8,9},{9,8},{10,11... | collective-permute-start | bytes 1572872 | tf_op jit(solution)/shard_map/ppermute | solution.py:186
  103.2 7.5 %collective-permute-start.19 = (bf16[128,512]{1,0:T(8,128)(2,1)S(1)}, bf16[128,512]{1,0:T(8,128)(2,1)S(1)}, u32[]{:S(2)}, u32[]{:S(2)}) collective-permute-start(bf16[128,512]{1,0:T(8,128)(2,1)S(1)} %pad_maximum_fusion.4), channel_id=1, source_target_pairs={{0,1},{1,0},{2,3},{3,2},{4,5},{5,4},{6,7},{7,6},{8,9},{9,8},{10,11... | collective-permute-start | bytes 393224 | tf_op jit(solution)/shard_map/ppermute | solution.py:186
  110.7 1.2 %maximum_select_fusion = bf16[128,4096]{1,0:T(8,128)(2,1)} fusion(bf16[128,2048]{1,0:T(8,128)(2,1)S(1)} %collective-permute-done.10, bf16[128,2048]{1,0:T(8,128)(2,1)S(1)} %copy-done, pred[]{:T(512)S(6)} %eq.4), kind=kLoop, calls=%fused_computation.1 | loop fusion | flops 4718592 | bytes 2097153 | tf_op jit(solution)/shard_map/jit(_where)/select_n | solution.py:195
  (82 shorter events, 8.1 us)
Async XLA Ops:
  1.6 2.3 %collective-permute-start.1 = (bf16[128,512]{1,0:T(8,128)(2,1)S(1)}, bf16[128,512]{1,0:T(8,128)(2,1)S(1)}, u32[]{:S(2)}, u32[]{:S(2)}) collective-permute-start(bf16[128,512]{1,0:T(8,128)(2,1)S(1)} %pad_maximum_fusion.3), channel_id=1, source_target_pairs={{0,1},{1,0},{2,3},{3,2},{4,5},{5,4},{6,7},{7,6},{8,9},{9,8},{10,11... | collective-permute-start | bytes 393224 | tf_op jit(solution)/shard_map/ppermute | solution.py:186
  3.8 34.2 %collective-permute-start = (bf16[128,4096]{1,0:T(8,128)(2,1)S(1)}, bf16[128,4096]{1,0:T(8,128)(2,1)S(1)}, u32[]{:S(2)}, u32[]{:S(2)}) collective-permute-start(bf16[128,4096]{1,0:T(8,128)(2,1)S(1)} %pad_maximum_fusion), channel_id=1, source_target_pairs={{0,1},{1,0},{2,3},{3,2},{4,5},{5,4},{6,7},{7,6},{8,9},{9,8},{10,11... | collective-permute-start | bytes 3145736 | tf_op jit(solution)/shard_map/ppermute | solution.py:186
  4.0 34.0 %copy-start.7 = (bf16[256,512]{1,0:T(8,128)(2,1)}, bf16[256,512]{1,0:T(8,128)(2,1)S(1)}, u32[]{:S(2)}) copy-start(bf16[256,512]{1,0:T(8,128)(2,1)S(1)} %fusion.5.c0) | copy-start | bytes 786436
  4.0 10.8 %collective-permute-start.5 = (bf16[256,512]{1,0:T(8,128)(2,1)S(1)}, bf16[256,512]{1,0:T(8,128)(2,1)S(1)}, u32[]{:S(2)}, u32[]{:S(2)}) collective-permute-start(bf16[256,512]{1,0:T(8,128)(2,1)S(1)} %fusion.5.c0), channel_id=1, source_target_pairs={{0,14},{1,15},{2,0},{3,1},{4,2},{5,3},{6,4},{7,5},{8,6},{9,7},{10,... | collective-permute-start | bytes 786440 | tf_op jit(solution)/shard_map/ppermute | solution.py:186
  9.6 8.6 %collective-permute-start.2 = (bf16[256,512]{1,0:T(8,128)(2,1)S(1)}, bf16[256,512]{1,0:T(8,128)(2,1)S(1)}, u32[]{:S(2)}, u32[]{:S(2)}) collective-permute-start(bf16[256,512]{1,0:T(8,128)(2,1)S(1)} %fusion.5.c0), channel_id=1, source_target_pairs={{0,2},{1,3},{2,4},{3,5},{4,6},{5,7},{6,8},{7,9},{8,10},{9,11},{10,... | collective-permute-start | bytes 786440 | tf_op jit(solution)/shard_map/ppermute | solution.py:186
  14.8 23.2 %copy-start.13 = (bf16[256,512]{1,0:T(8,128)(2,1)}, bf16[256,512]{1,0:T(8,128)(2,1)S(1)}, u32[]{:S(2)}) copy-start(bf16[256,512]{1,0:T(8,128)(2,1)S(1)} %collective-permute-done.5.d1) | copy-start | bytes 786436
  14.8 7.7 %collective-permute-start.6 = (bf16[256,512]{1,0:T(8,128)(2,1)S(1)}, bf16[256,512]{1,0:T(8,128)(2,1)S(1)}, u32[]{:S(2)}, u32[]{:S(2)}) collective-permute-start(bf16[256,512]{1,0:T(8,128)(2,1)S(1)} %collective-permute-done.5.d1), channel_id=1, source_target_pairs={{0,14},{1,15},{2,0},{3,1},{4,2},{5,3},{6,4},{7,5},{8,6},{9,7},{10,... | collective-permute-start | bytes 786440 | tf_op jit(solution)/shard_map/ppermute | solution.py:186
  18.2 7.7 %collective-permute-start.3 = (bf16[256,512]{1,0:T(8,128)(2,1)S(1)}, bf16[256,512]{1,0:T(8,128)(2,1)S(1)}, u32[]{:S(2)}, u32[]{:S(2)}) collective-permute-start(bf16[256,512]{1,0:T(8,128)(2,1)S(1)} %collective-permute-done.2.u1), channel_id=1, source_target_pairs={{0,2},{1,3},{2,4},{3,5},{4,6},{5,7},{6,8},{7,9},{8,10},{9,11},{10,... | collective-permute-start | bytes 786440 | tf_op jit(solution)/shard_map/ppermute | solution.py:186
  22.5 6.7 %collective-permute-start.7 = (bf16[256,512]{1,0:T(8,128)(2,1)S(1)}, bf16[256,512]{1,0:T(8,128)(2,1)S(1)}, u32[]{:S(2)}, u32[]{:S(2)}) collective-permute-start(bf16[256,512]{1,0:T(8,128)(2,1)S(1)} %collective-permute-done.6.d2), channel_id=1, source_target_pairs={{0,14},{1,15},{2,0},{3,1},{4,2},{5,3},{6,4},{7,5},{8,6},{9,7},{10,... | collective-permute-start | bytes 786440 | tf_op jit(solution)/shard_map/ppermute | solution.py:186
  25.9 6.8 %collective-permute-start.4 = (bf16[256,512]{1,0:T(8,128)(2,1)S(1)}, bf16[256,512]{1,0:T(8,128)(2,1)S(1)}, u32[]{:S(2)}, u32[]{:S(2)}) collective-permute-start(bf16[256,512]{1,0:T(8,128)(2,1)S(1)} %collective-permute-done.3.u2), channel_id=1, source_target_pairs={{0,2},{1,3},{2,4},{3,5},{4,6},{5,7},{6,8},{7,9},{8,10},{9,11},{10,... | collective-permute-start | bytes 786440 | tf_op jit(solution)/shard_map/ppermute | solution.py:186
  29.2 5.5 %collective-permute-start.9 = (bf16[256,256]{1,0:T(8,128)(2,1)S(1)}, bf16[256,256]{1,0:T(8,128)(2,1)S(1)}, u32[]{:S(2)}, u32[]{:S(2)}) collective-permute-start(bf16[256,256]{1,0:T(8,128)(2,1)S(1)} %slice.85), channel_id=1, source_target_pairs={{0,14},{1,15},{2,0},{3,1},{4,2},{5,3},{6,4},{7,5},{8,6},{9,7},{10,... | collective-permute-start | bytes 393224 | tf_op jit(solution)/shard_map/ppermute | solution.py:186
  32.8 5.2 %collective-permute-start.8 = (bf16[256,256]{1,0:T(8,128)(2,1)S(1)}, bf16[256,256]{1,0:T(8,128)(2,1)}, u32[]{:S(2)}, u32[]{:S(2)}) collective-permute-start(bf16[256,256]{1,0:T(8,128)(2,1)S(1)} %slice.84), channel_id=1, source_target_pairs={{0,2},{1,3},{2,4},{3,5},{4,6},{5,7},{6,8},{7,9},{8,10},{9,11},{10,... | collective-permute-start | bytes 393224 | tf_op jit(solution)/shard_map/ppermute | solution.py:186
  51.9 23.9 %copy-start.5 = (bf16[256,512]{1,0:T(8,128)(2,1)S(1)}, bf16[256,512]{1,0:T(8,128)(2,1)}, u32[]{:S(2)}) copy-start(bf16[256,512]{1,0:T(8,128)(2,1)} %get-tuple-element.18) | copy-start | bytes 786436
  52.9 17.8 %collective-permute-start.15 = (bf16[256,256]{1,0:T(8,128)(2,1)S(1)}, bf16[256,256]{1,0:T(8,128)(2,1)S(1)}, u32[]{:S(2)}, u32[]{:S(2)}) collective-permute-start(bf16[256,256]{1,0:T(8,128)(2,1)S(1)} %get-tuple-element.28), channel_id=1, source_target_pairs={{0,14},{1,15},{2,0},{3,1},{4,2},{5,3},{6,4},{7,5},{8,6},{9,7},{10,... | collective-permute-start | bytes 393224 | tf_op jit(solution)/shard_map/ppermute | solution.py:186
  70.7 5.1 %collective-permute-start.11 = (bf16[256,256]{1,0:T(8,128)(2,1)S(1)}, bf16[256,256]{1,0:T(8,128)(2,1)S(1)}, u32[]{:S(2)}, u32[]{:S(2)}) collective-permute-start(bf16[256,256]{1,0:T(8,128)(2,1)S(1)} %get-tuple-element.27), channel_id=1, source_target_pairs={{0,2},{1,3},{2,4},{3,5},{4,6},{5,7},{6,8},{7,9},{8,10},{9,11},{10,... | collective-permute-start | bytes 393224 | tf_op jit(solution)/shard_map/ppermute | solution.py:186
  70.8 7.4 %collective-permute-start.16 = (bf16[256,512]{1,0:T(8,128)(2,1)S(1)}, bf16[256,512]{1,0:T(8,128)(2,1)S(1)}, u32[]{:S(2)}, u32[]{:S(2)}) collective-permute-start(bf16[256,512]{1,0:T(8,128)(2,1)S(1)} %pad_maximum_fusion.2), channel_id=1, source_target_pairs={{0,14},{1,15},{2,0},{3,1},{4,2},{5,3},{6,4},{7,5},{8,6},{9,7},{10,... | collective-permute-start | bytes 786440 | tf_op jit(solution)/shard_map/ppermute | solution.py:186
  75.8 7.8 %collective-permute-start.12 = (bf16[256,512]{1,0:T(8,128)(2,1)S(1)}, bf16[256,512]{1,0:T(8,128)(2,1)S(1)}, u32[]{:S(2)}, u32[]{:S(2)}) collective-permute-start(bf16[256,512]{1,0:T(8,128)(2,1)S(1)} %pad_maximum_fusion.1), channel_id=1, source_target_pairs={{0,2},{1,3},{2,4},{3,5},{4,6},{5,7},{6,8},{7,9},{8,10},{9,11},{10,... | collective-permute-start | bytes 786440 | tf_op jit(solution)/shard_map/ppermute | solution.py:186
  78.3 8.7 %collective-permute-start.17 = (bf16[256,512]{1,0:T(8,128)(2,1)S(1)}, bf16[256,512]{1,0:T(8,128)(2,1)S(1)}, u32[]{:S(2)}, u32[]{:S(2)}) collective-permute-start(bf16[256,512]{1,0:T(8,128)(2,1)S(1)} %add_convert_fusion.2), channel_id=1, source_target_pairs={{0,14},{1,15},{2,0},{3,1},{4,2},{5,3},{6,4},{7,5},{8,6},{9,7},{10,... | collective-permute-start | bytes 786440 | tf_op jit(solution)/shard_map/ppermute | solution.py:186
  83.6 19.4 %copy-start.8 = (bf16[256,512]{1,0:T(8,128)(2,1)S(1)}, bf16[256,512]{1,0:T(8,128)(2,1)}, u32[]{:S(2)}) copy-start(bf16[256,512]{1,0:T(8,128)(2,1)} %get-tuple-element.15) | copy-start | bytes 786436
  83.7 8.9 %collective-permute-start.13 = (bf16[256,512]{1,0:T(8,128)(2,1)S(1)}, bf16[256,512]{1,0:T(8,128)(2,1)S(1)}, u32[]{:S(2)}, u32[]{:S(2)}) collective-permute-start(bf16[256,512]{1,0:T(8,128)(2,1)S(1)} %add_convert_fusion.4), channel_id=1, source_target_pairs={{0,2},{1,3},{2,4},{3,5},{4,6},{5,7},{6,8},{7,9},{8,10},{9,11},{10,... | collective-permute-start | bytes 786440 | tf_op jit(solution)/shard_map/ppermute | solution.py:186
  87.2 15.9 %collective-permute-start.18 = (bf16[256,512]{1,0:T(8,128)(2,1)S(1)}, bf16[256,512]{1,0:T(8,128)(2,1)S(1)}, u32[]{:S(2)}, u32[]{:S(2)}) collective-permute-start(bf16[256,512]{1,0:T(8,128)(2,1)S(1)} %add_convert_fusion.1), channel_id=1, source_target_pairs={{0,14},{1,15},{2,0},{3,1},{4,2},{5,3},{6,4},{7,5},{8,6},{9,7},{10,... | collective-permute-start | bytes 786440 | tf_op jit(solution)/shard_map/ppermute | solution.py:186
  92.7 10.3 %collective-permute-start.14 = (bf16[256,512]{1,0:T(8,128)(2,1)S(1)}, bf16[256,512]{1,0:T(8,128)(2,1)S(1)}, u32[]{:S(2)}, u32[]{:S(2)}) collective-permute-start(bf16[256,512]{1,0:T(8,128)(2,1)S(1)} %add_convert_fusion.3), channel_id=1, source_target_pairs={{0,2},{1,3},{2,4},{3,5},{4,6},{5,7},{6,8},{7,9},{8,10},{9,11},{10,... | collective-permute-start | bytes 786440 | tf_op jit(solution)/shard_map/ppermute | solution.py:186
  92.8 17.9 %collective-permute-start.10 = (bf16[128,2048]{1,0:T(8,128)(2,1)S(1)}, bf16[128,2048]{1,0:T(8,128)(2,1)S(1)}, u32[]{:S(2)}, u32[]{:S(2)}) collective-permute-start(bf16[128,2048]{1,0:T(8,128)(2,1)S(1)} %copy-done.12), channel_id=1, source_target_pairs={{0,1},{1,0},{2,3},{3,2},{4,5},{5,4},{6,7},{7,6},{8,9},{9,8},{10,11... | collective-permute-start | bytes 1572872 | tf_op jit(solution)/shard_map/ppermute | solution.py:186
  103.2 8.8 %collective-permute-start.19 = (bf16[128,512]{1,0:T(8,128)(2,1)S(1)}, bf16[128,512]{1,0:T(8,128)(2,1)S(1)}, u32[]{:S(2)}, u32[]{:S(2)}) collective-permute-start(bf16[128,512]{1,0:T(8,128)(2,1)S(1)} %pad_maximum_fusion.4), channel_id=1, source_target_pairs={{0,1},{1,0},{2,3},{3,2},{4,5},{5,4},{6,7},{7,6},{8,9},{9,8},{10,11... | collective-permute-start | bytes 393224 | tf_op jit(solution)/shard_map/ppermute | solution.py:186
  (14 other events, 129.6 us)
